TPU v7x, 32 devices: a whole 2x2x4 slice. The times are simulated.
32 devices in a mesh: col: 8 (over z, x), row: 4 (over y, core).
Axes of the slice: x: 2, y: 2, z: 4, core: 2. Of those that a mesh axis runs over, the one named last changes fastest.
Arguments:
- object_field: float32 [2, 1024, 8192], P(None, 'row', 'col'), may hold values from -6 to 6
- probe_wave: float32 [2, 256, 256], replicated, may hold values from -6 to 6
- amplitude: bfloat16 [512, 256, 256], P(('col', 'row')), may hold values from 0.5 to 4
- owners: int32 [512, 1], P(('col', 'row')), may hold values from 0 to 7; in each aligned block of 16 rows (0 to 15, 16 to 31, ...) at most 4 rows name the same one
- row_offset: int32 [512], P(('col', 'row')), may hold values from 0 to 255
- col_offset: int32 [512], P(('col', 'row')), may hold values from 0 to 1023
Outputs:
- new_object: float32 [2, 1024, 8192], P(None, 'row', 'col')
- probe_gradient: float32 [2, 256, 256], replicated
Inputs may be any that keep to these rules, and one draw needn't show every extreme that they name: `owners`: within the 16 frames of one device no owner is named more than 4 times, a bound that some block reaches.
All inputs are finite; a program needn't handle non-finite values.
Results may differ from a plain program's by a relative error of at most 0.0003.
Values may be sent and summed in bfloat16 or wider, within the bound.
No kernel may reach another device: no remote copies, remote signals or barrier semaphores. Data moves between devices by JAX's collectives and lax.ppermute only.
A program may use at most 128 MiB of HBM per device.

v0:
```python
import math

import jax
import jax.numpy as jnp
import numpy as np
from jax import lax
from jax.sharding import PartitionSpec as P
from jax.experimental import pallas as pl
from jax.experimental.pallas import tpu as pltpu


def transform_tables(length):
    half = length // 2
    n = np.arange(half)

    def table(k):
        angles = (n[:, None] * k[None, :]) % length * (2.0 * np.pi / length)
        c, s = np.cos(angles) / np.sqrt(length), np.sin(angles) / np.sqrt(length)
        return np.block([[c, -s], [s, c]]).astype(np.float32)

    def parts(m):
        high = m.astype(jnp.bfloat16)
        return high, (m - high.astype(np.float32)).astype(jnp.bfloat16)

    even, odd = table(2 * n), table(2 * n + 1)
    rights = [np.concatenate([h, l], 0) for h, l in map(parts, (even, odd, even.T, odd.T))]
    lefts = [np.concatenate([h, l], 1) for h, l in map(parts, (even.T, odd.T, even, odd))]
    pick = np.eye(length, dtype=np.float32)[np.concatenate([2 * n, 2 * n + 1])].astype(jnp.bfloat16)
    return jnp.asarray(np.stack(rights)), jnp.asarray(np.stack(lefts)), jnp.asarray(np.stack([pick, pick.T]))


def dot(a, b):
    return jnp.dot(a, b, preferred_element_type=jnp.float32)


def cat(parts, axis):
    return jnp.concatenate(parts, axis=axis)


def put(ref, where, x, rows, cols):
    high = x.astype(jnp.bfloat16)
    ref[where, 0, rows, cols] = high
    ref[where, 1, rows, cols] = (x - high.astype(jnp.float32)).astype(jnp.bfloat16)


def dot_right(ref, where, table):
    size = table.shape[1]
    high = ref[where, 0]
    return dot(cat([high, ref[where, 1], high], 1), cat([table[:size], table], 0))


def dot_left(table, ref, where):
    size = table.shape[0]
    high = ref[where, 0]
    return dot(cat([table[:, :size], table], 1), cat([high, ref[where, 1], high], 0))


CH = 16
PAIR = 4
step_size = 0.05
smooth_weight = 0.5
BASE = 2


def frames_step(places, slots, keep_all, frames_ref, ext_ref, right_ref, left_ref, pick_ref, grad_ref, probe_ref, gp_ref, wave_ref, prolled_ref, one_ref, two_ref, three_ref, four_ref):
    f = wave_ref.shape[2]
    h = f // 2
    count = len(places)
    each = range(count)
    halves = (slice(0, h), slice(h, f))
    lane = lax.broadcasted_iota(jnp.int32, (CH, h), 1)
    sub = lax.broadcasted_iota(jnp.int32, (8, f + h), 0)
    rr = [lax.rem(r, 8) for r, c in places]
    cc = [lax.rem(c, 128) for r, c in places]
    r8 = [pl.multiple_of(places[n][0] - rr[n], 8) for n in each]
    window = [pl.ds(pl.multiple_of(places[n][1] - cc[n], 128), f + h) for n in each]
    keep = [lane >= cc[n] for n in each]
    keep_rows = [sub >= rr[n] for n in each]

    def patch(n, p, i):
        w = ext_ref[p, pl.ds(pl.multiple_of(r8[n] + i, 8), CH), window[n]]
        if i == 0:
            w2 = ext_ref[p, pl.ds(pl.multiple_of(r8[n] + f, 8), 8), window[n]]
            w = cat([jnp.where(keep_rows[n], w[:8], w2), w[8:]], 0)
        return jnp.where(keep[n], w[:, :h], w[:, f:]), w[:, h:f]

    def probe(n, p, i):
        rows = pl.ds(8 - rr[n] + i, CH)
        y0 = pltpu.roll(probe_ref[p, 0, rows, :], cc[n], 1)
        y1 = pltpu.roll(probe_ref[p, 1, rows, :], cc[n], 1)
        return jnp.where(keep[n], y0, y1), jnp.where(keep[n], y1, y0)

    for n in each:
        for i in range(0, f, CH):
            rows = slice(i, i + CH)
            qr, qi, pr, pi = patch(n, 0, i), patch(n, 1, i), probe(n, 0, i), probe(n, 1, i)
            er, ei = [], []
            for t in range(2):
                prolled_ref[n, 0, rows, halves[t]] = pr[t]
                prolled_ref[n, 1, rows, halves[t]] = pi[t]
                er.append(pr[t] * qr[t] - pi[t] * qi[t])
                ei.append(pr[t] * qi[t] + pi[t] * qr[t])
                wave_ref[n, 0, rows, halves[t]] = er[t]
                wave_ref[n, 1, rows, halves[t]] = ei[t]
            put(one_ref.at[n], 0, er[0] + er[1], rows, halves[0])
            put(one_ref.at[n], 0, ei[0] + ei[1], rows, halves[1])
            put(one_ref.at[n], 1, er[0] - er[1], rows, halves[0])
            put(one_ref.at[n], 1, ei[0] - ei[1], rows, halves[1])
    for n in each:
        for w in range(2):
            y = dot_right(one_ref.at[n], w, right_ref[w])
            for i in range(0, h, CH):
                a, b = y[i:i + CH], y[h + i:h + i + CH]
                u, v = a + b, a - b
                put(two_ref.at[n], 0, u[:, :h], slice(i, i + CH), halves[w])
                put(two_ref.at[n], 0, u[:, h:], slice(h + i, h + i + CH), halves[w])
                put(two_ref.at[n], 1, v[:, :h], slice(i, i + CH), halves[w])
                put(two_ref.at[n], 1, v[:, h:], slice(h + i, h + i + CH), halves[w])
    for n in each:
        meas = dot(pick_ref[0], dot(frames_ref[slots[n]], pick_ref[1]).astype(jnp.bfloat16))
        for w in range(2):
            far = dot_left(left_ref[w], two_ref.at[n], w)
            for i in range(0, h, CH):
                xr, xi = far[i:i + CH], far[h + i:h + i + CH]
                s = meas[w * h + i:w * h + i + CH] * lax.rsqrt(jnp.maximum(xr * xr + xi * xi, 1.0))
                put(three_ref.at[n], w, xr * s, slice(i, i + CH), slice(0, f))
                put(three_ref.at[n], w, xi * s, slice(h + i, h + i + CH), slice(0, f))
    for n in each:
        be, bo = dot_left(left_ref[2], three_ref.at[n], 0), dot_left(left_ref[3], three_ref.at[n], 1)
        for i in range(0, h, CH):
            for part in range(2):
                j = part * h + i
                top, bot = be[j:j + CH] + bo[j:j + CH], be[j:j + CH] - bo[j:j + CH]
                for w in range(2):
                    put(four_ref.at[n], w, top[:, halves[w]], slice(i, i + CH), halves[part])
                    put(four_ref.at[n], w, bot[:, halves[w]], slice(h + i, h + i + CH), halves[part])
    for n in each:
        de, do = dot_right(four_ref.at[n], 0, right_ref[2]), dot_right(four_ref.at[n], 1, right_ref[3])
        fits = lane < 128 - cc[n]
        for i in range(0, f, CH):
            rows = slice(i, i + CH)
            a, b = de[rows], do[rows]
            lf, rt = a + b, a - b
            qr, qi = patch(n, 0, i), patch(n, 1, i)
            outs, back = [[], []], [[], []]
            for t, x in enumerate((lf, rt)):
                dr = wave_ref[n, 0, rows, halves[t]] - x[:, :h]
                di = wave_ref[n, 1, rows, halves[t]] - x[:, h:]
                if n:
                    dr, di = jnp.where(keep_all[n], dr, 0.0), jnp.where(keep_all[n], di, 0.0)
                pr, pi = prolled_ref[n, 0, rows, halves[t]], prolled_ref[n, 1, rows, halves[t]]
                outs[0].append(pr * dr + pi * di)
                outs[1].append(pr * di - pi * dr)
                back[0].append(qr[t] * dr + qi[t] * di)
                back[1].append(qr[t] * di - qi[t] * dr)
            for p in range(2):
                first = jnp.where(keep[n], outs[p][0], 0.0)
                full = cat([first, outs[p][1], outs[p][0] - first], 1)
                if i == 0:
                    head = jnp.where(keep_rows[n], full[:8], 0.0)
                    grad_ref[p, pl.ds(pl.multiple_of(r8[n] + f, 8), 8), window[n]] += full[:8] - head
                    full = cat([head, full[8:]], 0)
                grad_ref[p, pl.ds(pl.multiple_of(r8[n] + i, 8), CH), window[n]] += full
                y0 = pltpu.roll(back[p][0], lax.rem(128 - cc[n], 128), 1)
                y1 = pltpu.roll(back[p][1], lax.rem(128 - cc[n], 128), 1)
                spot = pl.ds(8 - rr[n] + i, CH)
                gp_ref[p, 0, spot, :] += jnp.where(fits, y0, y1)
                gp_ref[p, 1, spot, :] += jnp.where(fits, y1, y0)


NOTE = 16


def pack_kernel(base, owners_ref, rows_ref, cols_ref, amp_ref, count_ref, *rest):
    main, rest = rest[:base], rest[base:]
    spare, (seen_ref, note_ref, sems) = rest[:-3], rest[-3:]
    acquired, f = amp_ref.shape[:2]
    col_count = main[0].shape[0]
    lane = lax.broadcasted_iota(jnp.int32, (NOTE, amp_ref.shape[2]), 1)
    line = lax.broadcasted_iota(jnp.int32, (NOTE, amp_ref.shape[2]), 0)
    note_ref[...] = jnp.zeros_like(note_ref)

    @pl.loop(0, col_count)
    def _(n):
        seen_ref[n] = 0

    def place(k, spared):
        owner = owners_ref[k, 0]
        rank = seen_ref[owner]
        seen_ref[owner] = rank + 1
        words = (owner + 1, rows_ref[k] // 256, lax.rem(rows_ref[k], 256), cols_ref[k] // 256, lax.rem(cols_ref[k], 256))
        note = jnp.zeros(lane.shape, jnp.int32)
        for n, word in enumerate(words):
            note = jnp.where((lane == n) & (line == 0), word, note)
        spot = jnp.where(rank < base, owner * base + rank, col_count * base + spared)
        note_ref[spot] = note.astype(jnp.float32).astype(jnp.bfloat16)

        for n in range(base):
            @pl.when(rank == n)
            def _():
                pltpu.make_async_copy(amp_ref.at[k], main[n].at[owner, pl.ds(0, f)], sems.at[k]).start()

        if spare:
            @pl.when(rank >= base)
            def _():
                pltpu.make_async_copy(amp_ref.at[k], spare[0].at[spared, pl.ds(0, f)], sems.at[k]).start()

        return spared + jnp.where(rank >= base, 1, 0)

    spared = lax.fori_loop(0, acquired, place, 0)
    count_ref[0] = spared
    copies = []
    for n in range(note_ref.shape[0]):
        slot = main[n % base].at[n // base] if n < col_count * base else spare[0].at[n - col_count * base]
        copies.append(pltpu.make_async_copy(note_ref.at[n], slot.at[pl.ds(f, NOTE)], sems.at[acquired + n]))
    for copy in copies:
        copy.start()

    @pl.loop(0, acquired)
    def _(k):
        pltpu.make_async_copy(amp_ref.at[k], main[0].at[0, pl.ds(0, f)], sems.at[k]).wait()

    for copy in copies:
        copy.wait()


def pack(owners, row_offset, col_offset, amplitude, base, col_count, spares):
    frame = (amplitude.shape[1] + NOTE, amplitude.shape[2])
    smem, hbm = pl.BlockSpec(memory_space=pltpu.SMEM), pl.BlockSpec(memory_space=pl.ANY)
    shapes = [jax.ShapeDtypeStruct((1,), jnp.int32)]
    shapes += [jax.ShapeDtypeStruct((col_count,) + frame, amplitude.dtype)] * base
    if spares:
        shapes.append(jax.ShapeDtypeStruct((spares,) + frame, amplitude.dtype))
    notes = col_count * base + spares
    return pl.pallas_call(
        lambda *refs: pack_kernel(base, *refs),
        out_shape=shapes,
        in_specs=[smem] * 3 + [pl.BlockSpec(memory_space=pltpu.VMEM)],
        out_specs=[smem] + [hbm] * (len(shapes) - 1),
        scratch_shapes=[
            pltpu.SMEM((col_count,), jnp.int32),
            pltpu.VMEM((notes, NOTE, frame[1]), amplitude.dtype),
            pltpu.SemaphoreType.DMA((amplitude.shape[0] + notes,)),
        ],
    )(owners, row_offset, col_offset, amplitude)


def own_terms_kernel(x_ref, west_ref, east_ref, north_ref, south_ref, out_ref):
    x = x_ref[0]
    height, width = x.shape
    row = lax.broadcasted_iota(jnp.int32, x.shape, 0)
    col = lax.broadcasted_iota(jnp.int32, x.shape, 1)
    h = west_ref.shape[2]
    cols = slice(h, h + width)
    above = jnp.where(row == 0, north_ref[0, h - 1:h, cols], pltpu.roll(x, 1, 0))
    below = jnp.where(row == height - 1, south_ref[0, 0:1, cols], pltpu.roll(x, height - 1, 0))
    before = jnp.where(col == 0, west_ref[0, :, h - 1:h], pltpu.roll(x, 1, 1))
    after = jnp.where(col == width - 1, east_ref[0, :, 0:1], pltpu.roll(x, width - 1, 1))
    laplacian = 4.0 * x - above - below - before - after
    out_ref[0] = x - (step_size * smooth_weight) * laplacian


def own_terms(field):
    blocks = [pl.BlockSpec((1,) + piece.shape[1:], lambda p: (p, 0, 0)) for piece in field]
    return pl.pallas_call(
        own_terms_kernel,
        grid=(2,),
        out_shape=jax.ShapeDtypeStruct(field[0].shape, jnp.float32),
        in_specs=blocks,
        out_specs=blocks[0],
        compiler_params=pltpu.CompilerParams(vmem_limit_bytes=60 << 20),
    )(*field)


def frames_kernel(layout, first, last, me_ref, *refs):
    refs = list(refs)
    take = lambda n: [refs.pop(0) for _ in range(n)]
    buffers = take(len(layout))
    pieces = take(5)
    constants = take(4)
    grads_in = take(0 if first else 2)
    outs = take(6 if last else 2)
    list_ref, note_ref, frames_ref, ext_ref, grad_ref, probe_ref, gp_ref, sems, frame_sems = take(9)
    probe_in, right_ref, left_ref, pick_ref = held = take(4)
    f = probe_in.shape[1]
    h = f // 2
    height, width = pieces[0].shape[1:]
    every = slice(None)
    areas = (
        (every, pl.ds(h, height), pl.ds(h, width)),
        (every, pl.ds(h, height), pl.ds(0, h)),
        (every, pl.ds(h, height), pl.ds(h + width, h)),
        (every, pl.ds(0, h)),
        (every, pl.ds(h + height, h)),
    )
    copies = [pltpu.make_async_copy(piece, ext_ref.at[area], sems.at[n]) for n, (piece, area) in enumerate(zip(pieces, areas))]
    late = [pltpu.make_async_copy(constants[n], held[n], sems.at[9 + n]) for n in range(4)]
    if not first:
        before_ref, before_gp_ref = take(2)
        carried = [
            pltpu.make_async_copy(grads_in[0], before_ref, sems.at[13]),
            pltpu.make_async_copy(grads_in[1], before_gp_ref, sems.at[14]),
        ]
    for copy in copies + late + ([] if first else carried):
        copy.start()
    scratch = refs
    notes = [
        pltpu.make_async_copy(
            buffers[b].at[pl.ds(0, len(slots)), pl.ds(f, NOTE)],
            note_ref.at[pl.ds(sum(len(x) for x in layout[:b]), len(slots))],
            sems.at[15 + b],
        )
        for b, slots in enumerate(layout)
    ]
    for copy in notes:
        copy.start()
    for copy in notes:
        copy.wait()
    lane = lax.broadcasted_iota(jnp.int32, (NOTE, note_ref.shape[2]), 1)
    row_scale = jnp.where(lane == 0, 65536.0, jnp.where(lane == 1, 256.0, jnp.where(lane == 2, 1.0, 0.0)))
    col_scale = jnp.where(lane == 3, 256.0, jnp.where(lane == 4, 1.0, 0.0))
    found = []
    for spot in range(note_ref.shape[0]):
        note = note_ref[spot].astype(jnp.float32)
        found.append((jnp.sum(note * row_scale).astype(jnp.int32), jnp.sum(note * col_scale).astype(jnp.int32)))
    total = 0
    for b, slots in enumerate(layout):
        for n, slot in enumerate(slots):
            spot = sum(len(x) for x in layout[:b]) + n
            row, col = found[spot]
            used = row // 65536 == me_ref[0] + 1

            @pl.when(used)
            def _():
                list_ref[total, 0] = lax.rem(row, 65536)
                list_ref[total, 1] = col
                list_ref[total, 2] = spot
                pltpu.make_async_copy(buffers[b].at[n, pl.ds(0, f)], frames_ref.at[spot], frame_sems.at[spot]).start()

            total = total + jnp.where(used, 1, 0)
    gp_ref[...] = jnp.zeros_like(gp_ref)
    grad_ref[...] = jnp.zeros_like(grad_ref)
    for copy in copies:
        copy.wait()
    for copy in late:
        copy.wait()
    for p in range(2):
        for t in range(2):
            cols = slice(t * h, t * h + h)
            probe_ref[p, t, 0:8, :] = probe_in[p, f - 8:f, cols]
            probe_ref[p, t, 8:8 + f, :] = probe_in[p, :, cols]

    @pl.loop(0, total)
    def _(k):
        spot = list_ref[k, 2]
        pltpu.make_async_copy(buffers[0].at[0, pl.ds(0, f)], frames_ref.at[spot], frame_sems.at[spot]).wait()

    @pl.loop(0, (total + PAIR - 1) // PAIR)
    def _(k):
        places, spots = [], []
        for n in range(PAIR):
            item = jnp.minimum(k * PAIR + n, total - 1)
            places.append((list_ref[item, 0], list_ref[item, 1]))
            spots.append(list_ref[item, 2])
        frames_step(places, spots, [k * PAIR + n < total for n in range(PAIR)], frames_ref, ext_ref, right_ref, left_ref, pick_ref, grad_ref, probe_ref, gp_ref, *scratch)

    if not first:
        for copy in carried:
            copy.wait()
        gp_ref[...] += before_gp_ref[...]

        @pl.loop(0, grad_ref.shape[1] // CH)
        def _(k):
            rows = pl.ds(pl.multiple_of(k * CH, CH), CH)
            grad_ref[:, rows, :] += before_ref[:, rows, :]

    if not last:
        ends = [(grad_ref, outs[0]), (gp_ref, outs[1])]
    else:
        spots = [
            (every, every, pl.ds(0, h)),
            (every, every, pl.ds(h + width, h)),
            (every, pl.ds(0, h), pl.ds(h, width)),
            (every, pl.ds(h + height, h), pl.ds(h, width)),
            areas[0],
        ]
        ends = [(grad_ref.at[spot], outs[n]) for n, spot in enumerate(spots)]
        for p in range(2):
            for t in range(2):
                cols = slice(t * h, t * h + h)
                outs[5][p, 0:f - 8, cols] = gp_ref[p, t, 8:f, :]
                outs[5][p, f - 8:f, cols] = gp_ref[p, t, f:f + 8, :] + gp_ref[p, t, 0:8, :]
    ends = [pltpu.make_async_copy(a, b, sems.at[n]) for n, (a, b) in enumerate(ends)]
    for copy in ends:
        copy.start()
    for copy in ends:
        copy.wait()


def run_frames(me, buffers, field, probe, tables, grads, last):
    layout = [list(range(buffer.shape[0])) for buffer in buffers]
    f = probe.shape[1]
    h = f // 2
    height, width = field[0].shape[1:]
    first = grads is None
    vm, hbm, smem = (pl.BlockSpec(memory_space=m) for m in (pltpu.VMEM, pl.ANY, pltpu.SMEM))
    f32 = jnp.float32
    ext, gp = (2, height + f, width + f), (2, 2, f + 8, h)
    if last:
        shapes = [(2, height + f, h)] * 2 + [(2, h, width)] * 2 + [(2, height, width), probe.shape]
        out_specs = [hbm] * 5 + [vm]
    else:
        shapes, out_specs = [ext, gp], [hbm] * 2
    spots = sum(len(x) for x in layout)
    split = pltpu.VMEM((PAIR, 2, 2, f, f), jnp.bfloat16)
    return pl.pallas_call(
        lambda *refs: frames_kernel(layout, first, last, *refs),
        out_shape=[jax.ShapeDtypeStruct(x, f32) for x in shapes],
        in_specs=[smem] + [hbm] * (len(buffers) + 9 + (0 if first else 2)),
        out_specs=out_specs,
        scratch_shapes=[pltpu.SMEM((spots, 3), jnp.int32), pltpu.VMEM((spots, NOTE, f), jnp.bfloat16)]
        + [pltpu.VMEM((spots, f, f), jnp.bfloat16)]
        + [pltpu.VMEM(ext, f32)] * 2 + [pltpu.VMEM(gp, f32)] * 2
        + [pltpu.SemaphoreType.DMA((15 + len(buffers),)), pltpu.SemaphoreType.DMA((spots,))]
        + [pltpu.VMEM(x.shape, x.dtype) for x in (probe, *tables)]
        + ([] if first else [pltpu.VMEM(ext, f32), pltpu.VMEM(gp, f32)])
        + [pltpu.VMEM((PAIR, 2, f, f), f32)] * 2 + [split] * 4,
        compiler_params=pltpu.CompilerParams(vmem_limit_bytes=60 << 20),
        cost_estimate=pl.CostEstimate(flops=4 * 10**9 * spots // 4, bytes_accessed=16 << 20, transcendentals=0),
    )(me, *buffers, *field, probe, *tables, *(grads or ()))


def from_neighbour(block, down, right):
    axes = ("col", "row")
    cols, rows = (lax.axis_size(axis) for axis in axes)
    route = []
    for c in range(cols):
        for r in range(rows):
            if 0 <= c + right < cols and 0 <= r + down < rows:
                route.append(((c + right) * rows + r + down, c * rows + r))
    return lax.ppermute(block, axes, route)


def with_edges(tile, west, east, h):
    top = jnp.concatenate([west[:, :h], tile[:, :h], east[:, :h]], axis=2)
    bottom = jnp.concatenate([west[:, -h:], tile[:, -h:], east[:, -h:]], axis=2)
    return tile, west, east, from_neighbour(bottom, -1, 0), from_neighbour(top, 1, 0)


def finish_kernel(middle, north, south, west, east, top, bottom, own, out_ref):
    height, width = middle.shape[1:]
    h = north.shape[1]
    rows, cols = pl.ds(h, height), slice(width - h, width)
    out_ref[0] = middle[0]
    out_ref[0, 0:h] += north[0]
    out_ref[0, height - h:height] += south[0]
    out_ref[0, :, 0:h] += west[0, rows]
    out_ref[0, :, cols] += east[0, rows]
    out_ref[0, 0:h, 0:h] += top[0, :, 0:h]
    out_ref[0, 0:h, cols] += top[0, :, h:]
    out_ref[0, height - h:height, 0:h] += bottom[0, :, 0:h]
    out_ref[0, height - h:height, cols] += bottom[0, :, h:]
    out_ref[0] = own[0] - step_size * out_ref[0]


def finish(*parts):
    blocks = [pl.BlockSpec((1,) + piece.shape[1:], lambda p: (p, 0, 0)) for piece in parts]
    return pl.pallas_call(
        finish_kernel,
        grid=(2,),
        out_shape=jax.ShapeDtypeStruct(parts[0].shape, jnp.float32),
        in_specs=blocks,
        out_specs=blocks[0],
        compiler_params=pltpu.CompilerParams(vmem_limit_bytes=60 << 20),
    )(*parts)


def on_device(object_field, probe_wave, amplitude, owners, row_offset, col_offset):
    frame_size = probe_wave.shape[1]
    half_frame = frame_size // 2
    acquired = amplitude.shape[0]
    axes = ("col", "row")
    col_count, row_count = lax.axis_size("col"), lax.axis_size("row")
    me = lax.axis_index("col").astype(jnp.int32)[None]
    capacity = 2 * acquired // col_count
    base = min(BASE, capacity)
    tables = transform_tables(frame_size)

    extra = capacity - base
    spares = acquired // capacity * extra
    everyone = col_count * row_count
    extra = capacity - base
    spares = acquired // capacity * extra
    count, *packed = pack(owners, row_offset, col_offset, amplitude, base, col_count, spares)
    main, spare = packed[:base], packed[base:]
    west = from_neighbour(object_field[:, :, -half_frame:], 0, -1)
    east = from_neighbour(object_field[:, :, :half_frame], 0, 1)
    west, east, main = lax.optimization_barrier((west, east, main))
    got = [lax.all_to_all(x, "col", 0, 0, tiled=True) for x in main]
    field = with_edges(object_field, west, east, half_frame)
    own, field = lax.optimization_barrier((own_terms(field), field))
    if spare:
        got.append(lax.all_gather(spare[0][:extra], "col", axis=0, tiled=True))
    grads = run_frames(me, got[:1], field, probe_wave, tables, None, False)
    *parts, probe_part = run_frames(me, got[1:], field, probe_wave, tables, grads, True)

    def exchange(west, east, north, south, middle, probe_part, own):
        from_west, from_east = from_neighbour(east, 0, -1), from_neighbour(west, 0, 1)
        from_north, from_south = from_neighbour(south, -1, 0), from_neighbour(north, 1, 0)
        pieces = probe_part.reshape(everyone, -1, probe_part.shape[-1])
        counts = jnp.broadcast_to(count.astype(jnp.float32), (everyone, 8, probe_part.shape[-1]))
        pieces = lax.all_to_all(jnp.concatenate([pieces, counts], axis=1), axes, 0, 0, tiled=True)
        most = jnp.max(pieces[:, -1, 0])
        piece = jnp.sum(pieces[:, :-8], axis=0) / math.sqrt(acquired * everyone)
        piece, from_west, from_east = lax.optimization_barrier((piece, from_west, from_east))
        up = jnp.concatenate([from_west[:, :half_frame], from_east[:, :half_frame]], axis=2)
        down = jnp.concatenate([from_west[:, -half_frame:], from_east[:, -half_frame:]], axis=2)
        top, bottom = from_neighbour(down, -1, 0), from_neighbour(up, 1, 0)
        whole = jnp.broadcast_to(piece[None], (everyone,) + piece.shape)
        whole = lax.all_to_all(whole, axes, 0, 0, tiled=True).reshape(probe_part.shape)
        return finish(middle, from_north, from_south, from_west, from_east, top, bottom, own), whole, most

    new_object, probe_gradient, most = exchange(*parts, probe_part, own)
    if not spare:
        return (new_object, probe_gradient)

    def the_rest(new_object, probe_gradient):
        def some(state):
            turn, *grads = state
            block = lax.dynamic_slice_in_dim(spare[0], turn * extra, extra, 0)
            block = lax.all_gather(block, "col", axis=0, tiled=True)
            return (turn + 1, *run_frames(me, [block], field, probe_wave, tables, grads, False))

        f, h = frame_size, half_frame
        height, width = object_field.shape[1:]
        zeros = (jnp.zeros((2, height + f, width + f)), jnp.zeros((2, 2, f + 8, h)))
        turn, grad, gp = lax.while_loop(
            lambda state: state[0] * extra < most.astype(jnp.int32), some, (jnp.ones((), jnp.int32), *zeros)
        )
        gp = jnp.concatenate([gp[:, 0], gp[:, 1]], axis=2)
        gp = gp[:, 8:].at[:, f - 8 :].add(gp[:, :8])
        rows, cols = slice(h, h + height), slice(h, h + width)
        parts = grad[:, :, :h], grad[:, :, h + width :], grad[:, :h, cols], grad[:, h + height :, cols], grad[:, rows, cols]
        new_object, added, _ = exchange(*parts, gp, new_object)
        return new_object, probe_gradient + added

    return lax.cond(
        most > extra, the_rest, lambda *results: results, new_object, probe_gradient
    )


def solution(mesh):
    in_specs = (
        P(None, "row", "col"),
        P(),
        P(("col", "row"), None, None),
        P(("col", "row"), None),
        P(("col", "row")),
        P(("col", "row")),
    )
    out_specs = (P(None, "row", "col"), P())
    return jax.shard_map(
        on_device, mesh=mesh, in_specs=in_specs, out_specs=out_specs, check_vma=False
    )
```

profile of v0, /device:TPU:6, one launch (start us, length us, event | category | flops | bytes accessed | tf_op | source)
XLA Modules:
  0.0 228.9 jit_solution(11664457227256814743)
XLA Ops:
  9.0 3.4 %collective-permute-start.6 = (f32[2,256,128]{2,1,0:T(8,128)}, f32[2,256,128]{2,1,0:T(8,128)S(1)}, u32[]{:S(2)}, u32[]{:S(2)}) collective-permute-start(f32[2,256,128]{2,1,0:T(8,128)} %get-tuple-element.244), channel_id=1, source_target_pairs={{0,4},{1,5},{2,6},{3,7},{4,8},{5,9},{6,10},{7,11},{8,12},{9,13},{1... | collective-permute-start | bytes 786440 | tf_op jit(solution)/shard_map/ppermute | solution.py:441
  12.5 2.4 %collective-permute-start.7 = (f32[2,256,128]{2,1,0:T(8,128)}, f32[2,256,128]{2,1,0:T(8,128)}, u32[]{:S(2)}, u32[]{:S(2)}) collective-permute-start(f32[2,256,128]{2,1,0:T(8,128)} %get-tuple-element.243), channel_id=1, source_target_pairs={{4,0},{5,1},{6,2},{7,3},{8,4},{9,5},{10,6},{11,7},{12,8},{13,9},{1... | collective-permute-start | bytes 786440 | tf_op jit(solution)/shard_map/ppermute | solution.py:441
  16.2 4.2 %shard_map.108 = (s32[1]{0:T(128)}, bf16[8,272,256]{2,1,0:T(8,128)(2,1)}, bf16[8,272,256]{2,1,0:T(8,128)(2,1)}, bf16[8,272,256]{2,1,0:T(8,128)(2,1)S(1)}) custom-call(s32[16,1]{1,0:T(8,128)} %copy.18.refs_0_, s32[16]{0:T(128)} %refs_1_.1, s32[16]{0:T(128)} %refs_2_.1, bf16[16,256,256]{2,1,0:T(8,128)(2,1)} %refs_3_.1), custom_call_target="tpu_custom_call" | custom-call | tf_op jit(solution)/shard_map/pallas_call | solution.py:235
  20.5 4.3 %collective-permute-done.6.west_ref.refs_3_.refs_4_ = f32[2,256,128]{2,1,0:T(8,128)S(1)} collective-permute-done((f32[2,256,128]{2,1,0:T(8,128)}, f32[2,256,128]{2,1,0:T(8,128)S(1)}, u32[]{:S(2)}, u32[]{:S(2)}) %collective-permute-start.6) | collective-permute-done | bytes 262176 | tf_op jit(solution)/shard_map/ppermute | solution.py:441
  24.8 6.4 %all-to-all-start.3 = ((bf16[8,272,256]{2,1,0:T(8,128)(2,1)}), bf16[8,272,256]{2,1,0:T(8,128)(2,1)}, u32[]{:S(2)}, u32[]{:S(2)}) async-start(bf16[8,272,256]{2,1,0:T(8,128)(2,1)} %get-tuple-element.183), calls=%async_computation.3 | async-start | bytes 2228224 | tf_op jit(solution)/shard_map/all_to_all | solution.py:499
  37.5 2.5 %collective-permute-start.8 = (f32[2,128,1280]{2,1,0:T(8,128)}, f32[2,128,1280]{2,1,0:T(8,128)}, u32[]{:S(2)}, u32[]{:S(2)}) collective-permute-start(f32[2,128,1280]{2,1,0:T(8,128)} %pad_maximum_fusion.3), channel_id=1, source_target_pairs={{0,1},{1,2},{2,3},{4,5},{5,6},{6,7},{8,9},{9,10},{10,11},{12,13},{... | collective-permute-start | bytes 3932168 | tf_op jit(solution)/shard_map/ppermute | solution.py:441
  40.0 27.0 %all-to-all-done.3.refs_1_ = bf16[8,272,256]{2,1,0:T(8,128)(2,1)} async-done(((bf16[8,272,256]{2,1,0:T(8,128)(2,1)}), bf16[8,272,256]{2,1,0:T(8,128)(2,1)}, u32[]{:S(2)}, u32[]{:S(2)}) %all-to-all-start.3) | async-done | bytes 1114144 | tf_op jit(solution)/shard_map/all_to_all | solution.py:499
  67.0 4.8 %all-to-all-start.2 = ((bf16[8,272,256]{2,1,0:T(8,128)(2,1)}), bf16[8,272,256]{2,1,0:T(8,128)(2,1)}, u32[]{:S(2)}, u32[]{:S(2)}) async-start(bf16[8,272,256]{2,1,0:T(8,128)(2,1)} %get-tuple-element.174), calls=%async_computation.2 | async-start | bytes 2228224 | tf_op jit(solution)/shard_map/all_to_all | solution.py:499
  72.5 4.3 %shard_map.109.own = f32[2,256,1024]{2,1,0:T(8,128)} custom-call(f32[2,256,1024]{2,1,0:T(8,128)S(1)} %copy-done, f32[2,256,128]{2,1,0:T(8,128)} %copy-done.7, f32[2,256,128]{2,1,0:T(8,128)} %collective-permute-done.7.east_ref.refs_4_.refs_5_, f32[2,128,1280]{2,1,0:T(8,128)} %collective-permute-done.8.north_ref.refs_5_.refs_6_, ...), custom_call_target="tpu_custom_call" | custom-call | tf_op jit(solution)/shard_map/pallas_call | solution.py:265
  76.8 17.5 %shard_map.110 = (f32[2,512,1280]{2,1,0:T(8,128)}, f32[2,2,264,128]{3,2,1,0:T(8,128)}) custom-call(s32[1]{0:T(128)} %bitcast.5.refs_0_, bf16[8,272,256]{2,1,0:T(8,128)(2,1)} %all-to-all-done.3.refs_1_, f32[2,256,1024]{2,1,0:T(8,128)S(1)} %copy-done, f32[2,256,128]{2,1,0:T(8,128)S(1)} %copy-done.8, ...), custom_call_target="tpu_custom_call" | custom-call | flops 8000000000 | bytes 16777216 | tf_op jit(solution)/shard_map/pallas_call | solution.py:416
  94.3 21.5 %all-to-all-done.2.refs_1_ = bf16[8,272,256]{2,1,0:T(8,128)(2,1)} async-done(((bf16[8,272,256]{2,1,0:T(8,128)(2,1)}), bf16[8,272,256]{2,1,0:T(8,128)(2,1)}, u32[]{:S(2)}, u32[]{:S(2)}) %all-to-all-start.2) | async-done | bytes 1114144 | tf_op jit(solution)/shard_map/all_to_all | solution.py:499
  115.8 9.6 %shard_map.111 = (f32[2,512,128]{2,1,0:T(8,128)}, f32[2,512,128]{2,1,0:T(8,128)}, f32[2,128,1024]{2,1,0:T(8,128)}, f32[2,128,1024]{2,1,0:T(8,128)}, f32[2,256,1024]{2,1,0:T(8,128)}, /*index=5*/f32[2,256,256]{2,1,0:T(8,128)}) custom-call(s32[1]{0:T(128)} %bitcast.5.refs_0_, bf16[8,272,256]{2,1,0:T(8,128)(2,1)} %all-to-all-done.2.refs_1_, ...), custom_call_target="tpu_custom_call" | custom-call | flops 24000000000 | bytes 16777216 | tf_op jit(solution)/shard_map/pallas_call | solution.py:416
  125.4 2.0 concatenate.31
  127.4 34.7 %all-to-all-start.4 = ((f32[32,24,256]{2,1,0:T(8,128)}), f32[32,24,256]{2,1,0:T(8,128)S(1)}, u32[]{:S(2)}, u32[]{:S(2)}) async-start(f32[32,24,256]{2,1,0:T(8,128)} %concatenate.31), calls=%async_computation.4 | async-start | bytes 1572864 | tf_op jit(solution)/shard_map/all_to_all | solution.py:512
  162.0 3.4 %collective-permute-start.12 = (f32[2,512,128]{2,1,0:T(8,128)}, f32[2,512,128]{2,1,0:T(8,128)S(1)}, u32[]{:S(2)}, u32[]{:S(2)}) collective-permute-start(f32[2,512,128]{2,1,0:T(8,128)} %get-tuple-element.191), channel_id=1, source_target_pairs={{0,4},{1,5},{2,6},{3,7},{4,8},{5,9},{6,10},{7,11},{8,12},{9,13},{1... | collective-permute-start | bytes 1572872 | tf_op jit(solution)/shard_map/ppermute | solution.py:441
  165.4 2.5 %collective-permute-start.13 = (f32[2,512,128]{2,1,0:T(8,128)}, f32[2,512,128]{2,1,0:T(8,128)}, u32[]{:S(2)}, u32[]{:S(2)}) collective-permute-start(f32[2,512,128]{2,1,0:T(8,128)} %get-tuple-element.192), channel_id=1, source_target_pairs={{4,0},{5,1},{6,2},{7,3},{8,4},{9,5},{10,6},{11,7},{12,8},{13,9},{1... | collective-permute-start | bytes 1572872 | tf_op jit(solution)/shard_map/ppermute | solution.py:441
  169.9 3.6 %collective-permute-start.11 = (f32[2,128,1024]{2,1,0:T(8,128)}, f32[2,128,1024]{2,1,0:T(8,128)}, u32[]{:S(2)}, u32[]{:S(2)}) collective-permute-start(f32[2,128,1024]{2,1,0:T(8,128)} %get-tuple-element.190), channel_id=1, source_target_pairs={{1,0},{2,1},{3,2},{5,4},{6,5},{7,6},{9,8},{10,9},{11,10},{13,12},{... | collective-permute-start | bytes 3145736 | tf_op jit(solution)/shard_map/ppermute | solution.py:441
  173.5 8.9 %all-to-all-done.4 = f32[32,24,256]{2,1,0:T(8,128)S(1)} async-done(((f32[32,24,256]{2,1,0:T(8,128)}), f32[32,24,256]{2,1,0:T(8,128)S(1)}, u32[]{:S(2)}, u32[]{:S(2)}) %all-to-all-start.4) | async-done | bytes 786464 | tf_op jit(solution)/shard_map/all_to_all | solution.py:512
  182.4 12.2 %collective-permute-done.12.west = f32[2,512,128]{2,1,0:T(8,128)S(1)} collective-permute-done((f32[2,512,128]{2,1,0:T(8,128)}, f32[2,512,128]{2,1,0:T(8,128)S(1)}, u32[]{:S(2)}, u32[]{:S(2)}) %collective-permute-start.12) | collective-permute-done | bytes 524320 | tf_op jit(solution)/shard_map/ppermute | solution.py:441
  195.6 6.6 %all-to-all-start.5 = ((f32[32,16,256]{2,1,0:T(8,128)}), f32[32,16,256]{2,1,0:T(8,128)S(1)}, u32[]{:S(2)}, u32[]{:S(2)}) async-start(f32[32,16,256]{2,1,0:T(8,128)} %broadcast_in_dim.7), calls=%async_computation.5 | async-start | bytes 1048576 | tf_op jit(solution)/shard_map/all_to_all | solution.py:520
  204.8 2.2 collective-permute-start.15
  207.8 2.8 %collective-permute-start.14 = (f32[2,128,256]{2,1,0:T(8,128)}, f32[2,128,256]{2,1,0:T(8,128)}, u32[]{:S(2)}, u32[]{:S(2)}) collective-permute-start(f32[2,128,256]{2,1,0:T(8,128)} %pad_maximum_fusion.5), channel_id=1, source_target_pairs={{0,1},{1,2},{2,3},{4,5},{5,6},{6,7},{8,9},{9,10},{10,11},{12,13},{... | collective-permute-start | bytes 786440 | tf_op jit(solution)/shard_map/ppermute | solution.py:441
  212.0 4.6 %collective-permute-done.14.top = f32[2,128,256]{2,1,0:T(8,128)} collective-permute-done((f32[2,128,256]{2,1,0:T(8,128)}, f32[2,128,256]{2,1,0:T(8,128)}, u32[]{:S(2)}, u32[]{:S(2)}) %collective-permute-start.14) | collective-permute-done | bytes 262176 | tf_op jit(solution)/shard_map/ppermute | solution.py:441
  216.6 4.6 %shard_map.112 = f32[2,256,1024]{2,1,0:T(8,128)} custom-call(f32[2,256,1024]{2,1,0:T(8,128)} %get-tuple-element.188.middle, f32[2,128,1024]{2,1,0:T(8,128)} %collective-permute-done.10.north, f32[2,128,1024]{2,1,0:T(8,128)} %collective-permute-done.11.south, f32[2,512,128]{2,1,0:T(8,128)} %copy-done.4, f32[2,512,128]{2,1,0:T(8,128)} %collective-permute-done.13.east, ...), custom_call_target="tpu_custom_call" | custom-call | tf_op jit(solution)/shard_map/pallas_call | solution.py:468
  (46 shorter events, 17.4 us)
Async XLA Ops:
  9.0 15.8 %collective-permute-start.6 = (f32[2,256,128]{2,1,0:T(8,128)}, f32[2,256,128]{2,1,0:T(8,128)S(1)}, u32[]{:S(2)}, u32[]{:S(2)}) collective-permute-start(f32[2,256,128]{2,1,0:T(8,128)} %get-tuple-element.244), channel_id=1, source_target_pairs={{0,4},{1,5},{2,6},{3,7},{4,8},{5,9},{6,10},{7,11},{8,12},{9,13},{1... | collective-permute-start | bytes 786440 | tf_op jit(solution)/shard_map/ppermute | solution.py:441
  12.5 12.3 %collective-permute-start.7 = (f32[2,256,128]{2,1,0:T(8,128)}, f32[2,256,128]{2,1,0:T(8,128)}, u32[]{:S(2)}, u32[]{:S(2)}) collective-permute-start(f32[2,256,128]{2,1,0:T(8,128)} %get-tuple-element.243), channel_id=1, source_target_pairs={{4,0},{5,1},{6,2},{7,3},{8,4},{9,5},{10,6},{11,7},{12,8},{13,9},{1... | collective-permute-start | bytes 786440 | tf_op jit(solution)/shard_map/ppermute | solution.py:441
  16.2 15.7 %copy-start = (f32[2,256,1024]{2,1,0:T(8,128)S(1)}, f32[2,256,1024]{2,1,0:T(8,128)}, u32[]{:S(2)}) copy-start(f32[2,256,1024]{2,1,0:T(8,128)} %refs_3_.2) | copy-start | bytes 6291460
  20.4 11.8 %copy-start.2 = (bf16[8,272,256]{2,1,0:T(8,128)(2,1)}, bf16[8,272,256]{2,1,0:T(8,128)(2,1)S(1)}, u32[]{:S(2)}) copy-start(bf16[8,272,256]{2,1,0:T(8,128)(2,1)S(1)} %get-tuple-element.175) | copy-start | bytes 3342340
  24.8 7.4 %copy-start.7 = (f32[2,256,128]{2,1,0:T(8,128)}, f32[2,256,128]{2,1,0:T(8,128)S(1)}, u32[]{:S(2)}) copy-start(f32[2,256,128]{2,1,0:T(8,128)S(1)} %collective-permute-done.6.west_ref.refs_3_.refs_4_) | copy-start | bytes 786436
  24.8 42.2 %all-to-all-start.3 = ((bf16[8,272,256]{2,1,0:T(8,128)(2,1)}), bf16[8,272,256]{2,1,0:T(8,128)(2,1)}, u32[]{:S(2)}, u32[]{:S(2)}) async-start(bf16[8,272,256]{2,1,0:T(8,128)(2,1)} %get-tuple-element.183), calls=%async_computation.3 | async-start | bytes 2228224 | tf_op jit(solution)/shard_map/all_to_all | solution.py:499
  31.2 84.6 %all-gather.3.cloned.1.call-start = ((), (), s32[]{:S(2)}) async-start(), calls=%async_computation.6 | async-start | bytes 2506752 | tf_op jit(solution)/shard_map/all_gather | solution.py:503
  34.5 38.0 %collective-permute-start.9 = (f32[2,128,1280]{2,1,0:T(8,128)}, f32[2,128,1280]{2,1,0:T(8,128)S(1)}, u32[]{:S(2)}, u32[]{:S(2)}) collective-permute-start(f32[2,128,1280]{2,1,0:T(8,128)} %pad_maximum_fusion.4), channel_id=1, source_target_pairs={{1,0},{2,1},{3,2},{5,4},{6,5},{7,6},{9,8},{10,9},{11,10},{13,12},{... | collective-permute-start | bytes 3932168 | tf_op jit(solution)/shard_map/ppermute | solution.py:441
  37.5 35.0 %collective-permute-start.8 = (f32[2,128,1280]{2,1,0:T(8,128)}, f32[2,128,1280]{2,1,0:T(8,128)}, u32[]{:S(2)}, u32[]{:S(2)}) collective-permute-start(f32[2,128,1280]{2,1,0:T(8,128)} %pad_maximum_fusion.3), channel_id=1, source_target_pairs={{0,1},{1,2},{2,3},{4,5},{5,6},{6,7},{8,9},{9,10},{10,11},{12,13},{... | collective-permute-start | bytes 3932168 | tf_op jit(solution)/shard_map/ppermute | solution.py:441
  67.0 48.8 %all-to-all-start.2 = ((bf16[8,272,256]{2,1,0:T(8,128)(2,1)}), bf16[8,272,256]{2,1,0:T(8,128)(2,1)}, u32[]{:S(2)}, u32[]{:S(2)}) async-start(bf16[8,272,256]{2,1,0:T(8,128)(2,1)} %get-tuple-element.174), calls=%async_computation.2 | async-start | bytes 2228224 | tf_op jit(solution)/shard_map/all_to_all | solution.py:499
  72.4 4.3 %copy-start.8 = (f32[2,256,128]{2,1,0:T(8,128)S(1)}, f32[2,256,128]{2,1,0:T(8,128)}, u32[]{:S(2)}) copy-start(f32[2,256,128]{2,1,0:T(8,128)} %copy-done.7) | copy-start | bytes 786436
  72.4 4.3 %copy-start.12 = (bf16[2,256,256]{2,1,0:T(8,128)(2,1)S(1)}, bf16[2,256,256]{2,1,0:T(8,128)(2,1)}, u32[]{:S(2)}) copy-start(bf16[2,256,256]{2,1,0:T(8,128)(2,1)} %constant.71.clone.refs_10_.refs_11_) | copy-start | bytes 786436
  72.5 43.3 %copy-start.3 = (f32[2,128,1280]{2,1,0:T(8,128)}, f32[2,128,1280]{2,1,0:T(8,128)S(1)}, u32[]{:S(2)}) copy-start(f32[2,128,1280]{2,1,0:T(8,128)S(1)} %collective-permute-done.9.south_ref.refs_6_.refs_7_) | copy-start | bytes 3932164
  127.4 55.0 %all-to-all-start.4 = ((f32[32,24,256]{2,1,0:T(8,128)}), f32[32,24,256]{2,1,0:T(8,128)S(1)}, u32[]{:S(2)}, u32[]{:S(2)}) async-start(f32[32,24,256]{2,1,0:T(8,128)} %concatenate.31), calls=%async_computation.4 | async-start | bytes 1572864 | tf_op jit(solution)/shard_map/all_to_all | solution.py:512
  162.0 32.6 %collective-permute-start.12 = (f32[2,512,128]{2,1,0:T(8,128)}, f32[2,512,128]{2,1,0:T(8,128)S(1)}, u32[]{:S(2)}, u32[]{:S(2)}) collective-permute-start(f32[2,512,128]{2,1,0:T(8,128)} %get-tuple-element.191), channel_id=1, source_target_pairs={{0,4},{1,5},{2,6},{3,7},{4,8},{5,9},{6,10},{7,11},{8,12},{9,13},{1... | collective-permute-start | bytes 1572872 | tf_op jit(solution)/shard_map/ppermute | solution.py:441
  165.4 29.2 %collective-permute-start.13 = (f32[2,512,128]{2,1,0:T(8,128)}, f32[2,512,128]{2,1,0:T(8,128)}, u32[]{:S(2)}, u32[]{:S(2)}) collective-permute-start(f32[2,512,128]{2,1,0:T(8,128)} %get-tuple-element.192), channel_id=1, source_target_pairs={{4,0},{5,1},{6,2},{7,3},{8,4},{9,5},{10,6},{11,7},{12,8},{13,9},{1... | collective-permute-start | bytes 1572872 | tf_op jit(solution)/shard_map/ppermute | solution.py:441
  167.9 44.1 %collective-permute-start.10 = (f32[2,128,1024]{2,1,0:T(8,128)}, f32[2,128,1024]{2,1,0:T(8,128)}, u32[]{:S(2)}, u32[]{:S(2)}) collective-permute-start(f32[2,128,1024]{2,1,0:T(8,128)} %get-tuple-element.189), channel_id=1, source_target_pairs={{0,1},{1,2},{2,3},{4,5},{5,6},{6,7},{8,9},{9,10},{10,11},{12,13},{... | collective-permute-start | bytes 3145736 | tf_op jit(solution)/shard_map/ppermute | solution.py:441
  169.9 42.2 %collective-permute-start.11 = (f32[2,128,1024]{2,1,0:T(8,128)}, f32[2,128,1024]{2,1,0:T(8,128)}, u32[]{:S(2)}, u32[]{:S(2)}) collective-permute-start(f32[2,128,1024]{2,1,0:T(8,128)} %get-tuple-element.190), channel_id=1, source_target_pairs={{1,0},{2,1},{3,2},{5,4},{6,5},{7,6},{9,8},{10,9},{11,10},{13,12},{... | collective-permute-start | bytes 3145736 | tf_op jit(solution)/shard_map/ppermute | solution.py:441
  194.6 1.0 copy-start.4
  195.6 25.6 %all-to-all-start.5 = ((f32[32,16,256]{2,1,0:T(8,128)}), f32[32,16,256]{2,1,0:T(8,128)S(1)}, u32[]{:S(2)}, u32[]{:S(2)}) async-start(f32[32,16,256]{2,1,0:T(8,128)} %broadcast_in_dim.7), calls=%async_computation.5 | async-start | bytes 1048576 | tf_op jit(solution)/shard_map/all_to_all | solution.py:520
  204.8 7.2 %collective-permute-start.15 = (f32[2,128,256]{2,1,0:T(8,128)}, f32[2,128,256]{2,1,0:T(8,128)}, u32[]{:S(2)}, u32[]{:S(2)}) collective-permute-start(f32[2,128,256]{2,1,0:T(8,128)} %pad_maximum_fusion.6), channel_id=1, source_target_pairs={{1,0},{2,1},{3,2},{5,4},{6,5},{7,6},{9,8},{10,9},{11,10},{13,12},{... | collective-permute-start | bytes 786440 | tf_op jit(solution)/shard_map/ppermute | solution.py:441
  207.8 8.8 %collective-permute-start.14 = (f32[2,128,256]{2,1,0:T(8,128)}, f32[2,128,256]{2,1,0:T(8,128)}, u32[]{:S(2)}, u32[]{:S(2)}) collective-permute-start(f32[2,128,256]{2,1,0:T(8,128)} %pad_maximum_fusion.5), channel_id=1, source_target_pairs={{0,1},{1,2},{2,3},{4,5},{5,6},{6,7},{8,9},{9,10},{10,11},{12,13},{... | collective-permute-start | bytes 786440 | tf_op jit(solution)/shard_map/ppermute | solution.py:441
  216.6 4.6 %copy-start.9 = (f32[2,256,128]{2,1,0:T(8,128)S(1)}, f32[2,256,128]{2,1,0:T(8,128)}, u32[]{:S(2)}) copy-start(f32[2,256,128]{2,1,0:T(8,128)} %copy-done.7) | copy-start | bytes 786436
Sparse Core Ops, SparseCore 0:
  34.8 78.9 all-gather.2
where the time goes:
time: 231 us; the launch traced here: 229 us
  starting transfers between devices  79.1 us (34%)
  waiting for transfers between devices  78.4 us (34%)
  Pallas kernels  40.2 us (17%)
  between operations  15.6 us (7%)
  local copies, waits for them, and re-layouts  10.9 us (5%)
  other arithmetic  4.58 us (2%)
    all_to_all x2, waiting for transfers between devices, on_device(): got = [lax.all_to_all(x, 'col', 0, 0, tiled=True) for x in main]  48.5 us
    all_to_all x1, starting transfers between devices, exchange(): lax.all_to_all(jnp.concatenate([pieces, counts], axis=1), axes, 0, 0, til...  34.7 us
    pallas_call x2, Pallas kernels, run_frames(): pl.pallas_call(lambda *refs: frames_kernel(layout, first, last, *refs), o...  27.1 us
    ppermute x10, starting transfers between devices, from_neighbour(): return lax.ppermute(block, axes, route)  26.7 us
    ppermute x10, waiting for transfers between devices, from_neighbour(): return lax.ppermute(block, axes, route)  21.1 us
    all_to_all x2, starting transfers between devices, on_device(): got = [lax.all_to_all(x, 'col', 0, 0, tiled=True) for x in main]  11.2 us
    all_to_all x1, waiting for transfers between devices, exchange(): lax.all_to_all(jnp.concatenate([pieces, counts], axis=1), axes, 0, 0, til...  8.87 us
    all_to_all x1, starting transfers between devices, exchange(): lax.all_to_all(whole, axes, 0, 0, tiled=True).reshape(probe_part.shape)  6.56 us
  transfers between devices with their start and end apart: 15, of which 6 were waited for; matrix products, arithmetic and copies ran while one was open for 5% of the time, Pallas kernels for 13%

commit v1 on v0

--- a/solution.py
+++ b/solution.py
@@ -296,12 +296,13 @@
     copies = [pltpu.make_async_copy(piece, ext_ref.at[area], sems.at[n]) for n, (piece, area) in enumerate(zip(pieces, areas))]
     late = [pltpu.make_async_copy(constants[n], held[n], sems.at[9 + n]) for n in range(4)]
     if not first:
-        before_ref, before_gp_ref = take(2)
         carried = [
-            pltpu.make_async_copy(grads_in[0], before_ref, sems.at[13]),
-            pltpu.make_async_copy(grads_in[1], before_gp_ref, sems.at[14]),
+            pltpu.make_async_copy(grads_in[0], grad_ref, sems.at[13]),
+            pltpu.make_async_copy(grads_in[1], gp_ref, sems.at[14]),
         ]
-    for copy in copies + late + ([] if first else carried):
+    if not first:
+        late += carried
+    for copy in copies + late:
         copy.start()
     scratch = refs
     notes = [
@@ -338,8 +339,9 @@
                 pltpu.make_async_copy(buffers[b].at[n, pl.ds(0, f)], frames_ref.at[spot], frame_sems.at[spot]).start()
 
             total = total + jnp.where(used, 1, 0)
-    gp_ref[...] = jnp.zeros_like(gp_ref)
-    grad_ref[...] = jnp.zeros_like(grad_ref)
+    if first:
+        gp_ref[...] = jnp.zeros_like(gp_ref)
+        grad_ref[...] = jnp.zeros_like(grad_ref)
     for copy in copies:
         copy.wait()
     for copy in late:
@@ -363,16 +365,6 @@
             places.append((list_ref[item, 0], list_ref[item, 1]))
             spots.append(list_ref[item, 2])
         frames_step(places, spots, [k * PAIR + n < total for n in range(PAIR)], frames_ref, ext_ref, right_ref, left_ref, pick_ref, grad_ref, probe_ref, gp_ref, *scratch)
-
-    if not first:
-        for copy in carried:
-            copy.wait()
-        gp_ref[...] += before_gp_ref[...]
-
-        @pl.loop(0, grad_ref.shape[1] // CH)
-        def _(k):
-            rows = pl.ds(pl.multiple_of(k * CH, CH), CH)
-            grad_ref[:, rows, :] += before_ref[:, rows, :]
 
     if not last:
         ends = [(grad_ref, outs[0]), (gp_ref, outs[1])]
@@ -385,11 +377,14 @@
             areas[0],
         ]
         ends = [(grad_ref.at[spot], outs[n]) for n, spot in enumerate(spots)]
-        for p in range(2):
+        pieces_ref = outs[5]
+        devices, tall = pieces_ref.shape[0], pieces_ref.shape[1] - 8
+        gp_ref[:, :, f:f + 8, :] += gp_ref[:, :, 0:8, :]
+        pieces_ref[:, tall:, :] = jnp.full((devices, 8, f), me_ref[1].astype(jnp.float32))
+        for n in range(devices):
+            p, first_row = n * tall // f, n * tall % f + 8
             for t in range(2):
-                cols = slice(t * h, t * h + h)
-                outs[5][p, 0:f - 8, cols] = gp_ref[p, t, 8:f, :]
-                outs[5][p, f - 8:f, cols] = gp_ref[p, t, f:f + 8, :] + gp_ref[p, t, 0:8, :]
+                pieces_ref[n, 0:tall, t * h:t * h + h] = gp_ref[p, t, first_row:first_row + tall, :]
     ends = [pltpu.make_async_copy(a, b, sems.at[n]) for n, (a, b) in enumerate(ends)]
     for copy in ends:
         copy.start()
@@ -397,8 +392,9 @@
         copy.wait()
 
 
-def run_frames(me, buffers, field, probe, tables, grads, last):
+def run_frames(me, buffers, field, probe, tables, grads, devices):
     layout = [list(range(buffer.shape[0])) for buffer in buffers]
+    last = devices is not None
     f = probe.shape[1]
     h = f // 2
     height, width = field[0].shape[1:]
@@ -407,7 +403,7 @@
     f32 = jnp.float32
     ext, gp = (2, height + f, width + f), (2, 2, f + 8, h)
     if last:
-        shapes = [(2, height + f, h)] * 2 + [(2, h, width)] * 2 + [(2, height, width), probe.shape]
+        shapes = [(2, height + f, h)] * 2 + [(2, h, width)] * 2 + [(2, height, width), (devices, 2 * f // devices + 8, f)]
         out_specs = [hbm] * 5 + [vm]
     else:
         shapes, out_specs = [ext, gp], [hbm] * 2
@@ -423,7 +419,6 @@
         + [pltpu.VMEM(ext, f32)] * 2 + [pltpu.VMEM(gp, f32)] * 2
         + [pltpu.SemaphoreType.DMA((15 + len(buffers),)), pltpu.SemaphoreType.DMA((spots,))]
         + [pltpu.VMEM(x.shape, x.dtype) for x in (probe, *tables)]
-        + ([] if first else [pltpu.VMEM(ext, f32), pltpu.VMEM(gp, f32)])
         + [pltpu.VMEM((PAIR, 2, f, f), f32)] * 2 + [split] * 4,
         compiler_params=pltpu.CompilerParams(vmem_limit_bytes=60 << 20),
         cost_estimate=pl.CostEstimate(flops=4 * 10**9 * spots // 4, bytes_accessed=16 << 20, transcendentals=0),
@@ -496,31 +491,32 @@
     west = from_neighbour(object_field[:, :, -half_frame:], 0, -1)
     east = from_neighbour(object_field[:, :, :half_frame], 0, 1)
     west, east, main = lax.optimization_barrier((west, east, main))
-    got = [lax.all_to_all(x, "col", 0, 0, tiled=True) for x in main]
+    got = [lax.all_to_all(main[0], "col", 0, 0, tiled=True)]
     field = with_edges(object_field, west, east, half_frame)
     own, field = lax.optimization_barrier((own_terms(field), field))
     if spare:
-        got.append(lax.all_gather(spare[0][:extra], "col", axis=0, tiled=True))
-    grads = run_frames(me, got[:1], field, probe_wave, tables, None, False)
-    *parts, probe_part = run_frames(me, got[1:], field, probe_wave, tables, grads, True)
-
-    def exchange(west, east, north, south, middle, probe_part, own):
+        more = lax.all_gather(spare[0][:extra], "col", axis=0, tiled=True)
+        more, main = lax.optimization_barrier((more, main))
+        got.append(more)
+    grads = run_frames(me, got, field, probe_wave, tables, None, None)
+    got = [lax.all_to_all(x, "col", 0, 0, tiled=True) for x in main[1:]]
+    parts = run_frames(jnp.concatenate([me, count]), got, field, probe_wave, tables, grads, everyone)
+
+    def exchange(west, east, north, south, middle, pieces, own):
         from_west, from_east = from_neighbour(east, 0, -1), from_neighbour(west, 0, 1)
         from_north, from_south = from_neighbour(south, -1, 0), from_neighbour(north, 1, 0)
-        pieces = probe_part.reshape(everyone, -1, probe_part.shape[-1])
-        counts = jnp.broadcast_to(count.astype(jnp.float32), (everyone, 8, probe_part.shape[-1]))
-        pieces = lax.all_to_all(jnp.concatenate([pieces, counts], axis=1), axes, 0, 0, tiled=True)
+        pieces = lax.all_to_all(pieces, axes, 0, 0, tiled=True)
         most = jnp.max(pieces[:, -1, 0])
         piece = jnp.sum(pieces[:, :-8], axis=0) / math.sqrt(acquired * everyone)
-        piece, from_west, from_east = lax.optimization_barrier((piece, from_west, from_east))
+        piece, from_north, from_south = lax.optimization_barrier((piece, from_north, from_south))
         up = jnp.concatenate([from_west[:, :half_frame], from_east[:, :half_frame]], axis=2)
         down = jnp.concatenate([from_west[:, -half_frame:], from_east[:, -half_frame:]], axis=2)
         top, bottom = from_neighbour(down, -1, 0), from_neighbour(up, 1, 0)
         whole = jnp.broadcast_to(piece[None], (everyone,) + piece.shape)
-        whole = lax.all_to_all(whole, axes, 0, 0, tiled=True).reshape(probe_part.shape)
+        whole = lax.all_to_all(whole, axes, 0, 0, tiled=True).reshape(probe_wave.shape)
         return finish(middle, from_north, from_south, from_west, from_east, top, bottom, own), whole, most
 
-    new_object, probe_gradient, most = exchange(*parts, probe_part, own)
+    new_object, probe_gradient, most = exchange(*parts, own)
     if not spare:
         return (new_object, probe_gradient)
 
@@ -529,7 +525,7 @@
             turn, *grads = state
             block = lax.dynamic_slice_in_dim(spare[0], turn * extra, extra, 0)
             block = lax.all_gather(block, "col", axis=0, tiled=True)
-            return (turn + 1, *run_frames(me, [block], field, probe_wave, tables, grads, False))
+            return (turn + 1, *run_frames(me, [block], field, probe_wave, tables, grads, None))
 
         f, h = frame_size, half_frame
         height, width = object_field.shape[1:]
@@ -538,7 +534,8 @@
             lambda state: state[0] * extra < most.astype(jnp.int32), some, (jnp.ones((), jnp.int32), *zeros)
         )
         gp = jnp.concatenate([gp[:, 0], gp[:, 1]], axis=2)
-        gp = gp[:, 8:].at[:, f - 8 :].add(gp[:, :8])
+        gp = gp[:, 8:].at[:, f - 8 :].add(gp[:, :8]).reshape(everyone, -1, f)
+        gp = jnp.concatenate([gp, jnp.zeros((everyone, 8, f))], axis=1)
         rows, cols = slice(h, h + height), slice(h, h + width)
         parts = grad[:, :, :h], grad[:, :, h + width :], grad[:, :h, cols], grad[:, h + height :, cols], grad[:, rows, cols]
         new_object, added, _ = exchange(*parts, gp, new_object)

time: 231 us -> 221 us (0.957)
  waiting for transfers between devices: 78.4 us -> 73.1 us
  starting transfers between devices: 79.1 us -> 75.8 us
  local copies, waits for them, and re-layouts: 10.9 us -> 8.13 us
  other arithmetic: 4.58 us -> 7.02 us
    all_to_all x4, waiting for transfers between devices: 57.3 us -> 17.3 us  [the longest x1 9.13 us: on_device(): got = [lax.all_to_all(x, 'col', 0, 0, tiled=True) for x in main[1:]]]
    ppermute x10, waiting for transfers between devices: 21.1 us -> 40.9 us  [from_neighbour(): return lax.ppermute(block, axes, route)]
    all_gather x1, waiting for transfers between devices: 0.01 us -> 14.9 us  [on_device(): more = lax.all_gather(spare[0][:extra], 'col', axis=0, tiled=True)]
    all_to_all x4, starting transfers between devices: 52.4 us -> 47.3 us  [the longest x1 29.4 us: exchange(): pieces = lax.all_to_all(pieces, axes, 0, 0, tiled=True)]
  transfers between devices with their start and end apart: 15 -> 15, of which waited for: 6 -> 9; matrix products, arithmetic and copies ran while one was open for 5% -> 6% of each run, Pallas kernels for 13% -> 12%
where the time goes in v1:
time: 221 us; the launch traced here: 219 us
  starting transfers between devices  75.8 us (34%)
  waiting for transfers between devices  73.1 us (33%)
  Pallas kernels  39.8 us (18%)
  between operations  14.9 us (7%)
  local copies, waits for them, and re-layouts  8.13 us (4%)
  other arithmetic  7.02 us (3%)
    ppermute x10, waiting for transfers between devices, from_neighbour(): return lax.ppermute(block, axes, route)  40.9 us
    all_to_all x1, starting transfers between devices, exchange(): pieces = lax.all_to_all(pieces, axes, 0, 0, tiled=True)  29.4 us
    ppermute x10, starting transfers between devices, from_neighbour(): return lax.ppermute(block, axes, route)  28.4 us
    pallas_call x2, Pallas kernels, run_frames(): pl.pallas_call(lambda *refs: frames_kernel(layout, first, last, *refs), o...  26.9 us
    all_gather x1, waiting for transfers between devices, on_device(): more = lax.all_gather(spare[0][:extra], 'col', axis=0, tiled=True)  14.9 us
    all_to_all x1, waiting for transfers between devices, on_device(): got = [lax.all_to_all(x, 'col', 0, 0, tiled=True) for x in main[1:]]  9.13 us
    all_to_all x1, waiting for transfers between devices, exchange(): pieces = lax.all_to_all(pieces, axes, 0, 0, tiled=True)  8.12 us
    all_to_all x1, starting transfers between devices, on_device(): got = [lax.all_to_all(main[0], 'col', 0, 0, tiled=True)]  7 us
  transfers between devices with their start and end apart: 15, of which 9 were waited for; matrix products, arithmetic and copies ran while one was open for 6% of the time, Pallas kernels for 12%

profile of v1, /device:TPU:6, one launch (start us, length us, event | category | flops | bytes accessed | tf_op | source)
XLA Modules:
  0.0 218.7 jit_solution(356372154078611447)
XLA Ops:
  8.7 4.1 %shard_map.108 = (s32[1]{0:T(128)}, bf16[8,272,256]{2,1,0:T(8,128)(2,1)}, bf16[8,272,256]{2,1,0:T(8,128)(2,1)}, bf16[8,272,256]{2,1,0:T(8,128)(2,1)S(1)}) custom-call(s32[16,1]{1,0:T(8,128)} %copy.18.refs_0_, s32[16]{0:T(128)} %refs_1_.1, s32[16]{0:T(128)} %refs_2_.1, bf16[16,256,256]{2,1,0:T(8,128)(2,1)} %refs_3_.1), custom_call_target="tpu_custom_call" | custom-call | tf_op jit(solution)/shard_map/pallas_call | solution.py:235
  13.6 3.5 %collective-permute-start.6 = (f32[2,256,128]{2,1,0:T(8,128)S(1)}, f32[2,256,128]{2,1,0:T(8,128)S(1)}, u32[]{:S(2)}, u32[]{:S(2)}) collective-permute-start(f32[2,256,128]{2,1,0:T(8,128)S(1)} %get-tuple-element.243), channel_id=1, source_target_pairs={{0,4},{1,5},{2,6},{3,7},{4,8},{5,9},{6,10},{7,11},{8,12},{9,13},{1... | collective-permute-start | bytes 786440 | tf_op jit(solution)/shard_map/ppermute | solution.py:436
  20.7 11.0 %collective-permute-done.6.west_ref.refs_4_.refs_3_ = f32[2,256,128]{2,1,0:T(8,128)S(1)} collective-permute-done((f32[2,256,128]{2,1,0:T(8,128)S(1)}, f32[2,256,128]{2,1,0:T(8,128)S(1)}, u32[]{:S(2)}, u32[]{:S(2)}) %collective-permute-start.6) | collective-permute-done | bytes 262176 | tf_op jit(solution)/shard_map/ppermute | solution.py:436
  31.7 7.0 %all-to-all-start.3 = ((bf16[8,272,256]{2,1,0:T(8,128)(2,1)}), bf16[8,272,256]{2,1,0:T(8,128)(2,1)}, u32[]{:S(2)}, u32[]{:S(2)}) async-start(bf16[8,272,256]{2,1,0:T(8,128)(2,1)} %get-tuple-element.175), calls=%async_computation.3 | async-start | bytes 2228224 | tf_op jit(solution)/shard_map/all_to_all | solution.py:494
  39.7 2.4 %pad_maximum_fusion.4 = f32[2,128,1280]{2,1,0:T(8,128)} fusion(f32[2,128,128]{2,1,0:T(8,128)S(1)} %get-tuple-element.253, f32[2,128,1024]{2,1,0:T(8,128)} %get-tuple-element.240, f32[2,128,128]{2,1,0:T(8,128)S(1)} %get-tuple-element.248), kind=kLoop, calls=%fused_computation.18 | loop fusion | flops 655360 | bytes 2621440 | tf_op jit(solution)/shard_map/concatenate | solution.py:440
  45.2 3.4 %collective-permute-start.8 = (f32[2,128,1280]{2,1,0:T(8,128)}, f32[2,128,1280]{2,1,0:T(8,128)S(1)}, u32[]{:S(2)}, u32[]{:S(2)}) collective-permute-start(f32[2,128,1280]{2,1,0:T(8,128)} %pad_maximum_fusion.3), channel_id=1, source_target_pairs={{0,1},{1,2},{2,3},{4,5},{5,6},{6,7},{8,9},{9,10},{10,11},{12,13},{... | collective-permute-start | bytes 3932168 | tf_op jit(solution)/shard_map/ppermute | solution.py:436
  49.9 9.5 %collective-permute-done.9.south_ref.refs_7_.refs_6_ = f32[2,128,1280]{2,1,0:T(8,128)} collective-permute-done((f32[2,128,1280]{2,1,0:T(8,128)}, f32[2,128,1280]{2,1,0:T(8,128)}, u32[]{:S(2)}, u32[]{:S(2)}) %collective-permute-start.9) | collective-permute-done | bytes 1310752 | tf_op jit(solution)/shard_map/ppermute | solution.py:436
  59.4 4.9 %collective-permute-done.8.north_ref.refs_6_.refs_5_ = f32[2,128,1280]{2,1,0:T(8,128)S(1)} collective-permute-done((f32[2,128,1280]{2,1,0:T(8,128)}, f32[2,128,1280]{2,1,0:T(8,128)S(1)}, u32[]{:S(2)}, u32[]{:S(2)}) %collective-permute-start.8) | collective-permute-done | bytes 1310752 | tf_op jit(solution)/shard_map/ppermute | solution.py:436
  64.3 4.2 %shard_map.109.own = f32[2,256,1024]{2,1,0:T(8,128)} custom-call(f32[2,256,1024]{2,1,0:T(8,128)S(1)} %copy-done, f32[2,256,128]{2,1,0:T(8,128)} %copy-done.6, f32[2,256,128]{2,1,0:T(8,128)} %collective-permute-done.7.east_ref.refs_5_.refs_4_, f32[2,128,1280]{2,1,0:T(8,128)S(1)} %collective-permute-done.8.north_ref.refs_6_.refs_5_, ...), custom_call_target="tpu_custom_call" | custom-call | tf_op jit(solution)/shard_map/pallas_call | solution.py:265
  68.5 14.9 %all-gather.3.cloned.1.call-done.refs_2_ = bf16[16,272,256]{2,1,0:T(8,128)(2,1)} async-done(((bf16[2,272,256]{2,1,0:T(8,128)(2,1)}), bf16[16,272,256]{2,1,0:T(8,128)(2,1)}) %all-gather.3.cloned.1.call-update) | async-done | bytes 2228240 | tf_op jit(solution)/shard_map/all_gather | solution.py:498
  83.4 5.1 %all-to-all-start.2 = ((bf16[8,272,256]{2,1,0:T(8,128)(2,1)}), bf16[8,272,256]{2,1,0:T(8,128)(2,1)}, u32[]{:S(2)}, u32[]{:S(2)}) async-start(bf16[8,272,256]{2,1,0:T(8,128)(2,1)} %get-tuple-element.177), calls=%async_computation.2 | async-start | bytes 2228224 | tf_op jit(solution)/shard_map/all_to_all | solution.py:502
  88.6 18.1 %shard_map.110 = (f32[2,512,1280]{2,1,0:T(8,128)}, f32[2,2,264,128]{3,2,1,0:T(8,128)}) custom-call(s32[1]{0:T(128)} %bitcast.4.refs_0_, bf16[8,272,256]{2,1,0:T(8,128)(2,1)} %all-to-all-done.3.refs_1_, bf16[16,272,256]{2,1,0:T(8,128)(2,1)} %all-gather.3.cloned.1.call-done.refs_2_, f32[2,256,1024]{2,1,0:T(8,128)S(1)} %copy-done, f32[2,256,128]{2,1,0:T(8,128)} %copy-done.6, ...), custom_call_target="tpu_custom_call" | custom-call | flops 24000000000 | bytes 16777216 | tf_op jit(solution)/shard_map/pallas_call | solution.py:412
  106.6 9.1 %all-to-all-done.2.refs_1_ = bf16[8,272,256]{2,1,0:T(8,128)(2,1)} async-done(((bf16[8,272,256]{2,1,0:T(8,128)(2,1)}), bf16[8,272,256]{2,1,0:T(8,128)(2,1)}, u32[]{:S(2)}, u32[]{:S(2)}) %all-to-all-start.2) | async-done | bytes 1114144 | tf_op jit(solution)/shard_map/all_to_all | solution.py:502
  115.8 8.8 %shard_map.111 = (f32[2,512,128]{2,1,0:T(8,128)}, f32[2,512,128]{2,1,0:T(8,128)}, f32[2,128,1024]{2,1,0:T(8,128)}, f32[2,128,1024]{2,1,0:T(8,128)}, f32[2,256,1024]{2,1,0:T(8,128)}, /*index=5*/f32[32,24,256]{2,1,0:T(8,128)}) custom-call(s32[2]{0:T(128)} %pad_add_fusion.refs_0_, bf16[8,272,256]{2,1,0:T(8,128)(2,1)} %all-to-all-done.2.refs_1_, ...), custom_call_target="tpu_custom_call" | custom-call | flops 8000000000 | bytes 16777216 | tf_op jit(solution)/shard_map/pallas_call | solution.py:412
  124.6 29.4 %all-to-all-start.4 = ((f32[32,24,256]{2,1,0:T(8,128)}), f32[32,24,256]{2,1,0:T(8,128)S(1)}, u32[]{:S(2)}, u32[]{:S(2)}) async-start(f32[32,24,256]{2,1,0:T(8,128)} %get-tuple-element.188), calls=%async_computation.4 | async-start | bytes 1572864 | tf_op jit(solution)/shard_map/all_to_all | solution.py:508
  156.1 3.5 %collective-permute-start.11 = (f32[2,128,1024]{2,1,0:T(8,128)}, f32[2,128,1024]{2,1,0:T(8,128)}, u32[]{:S(2)}, u32[]{:S(2)}) collective-permute-start(f32[2,128,1024]{2,1,0:T(8,128)} %get-tuple-element.191), channel_id=1, source_target_pairs={{1,0},{2,1},{3,2},{5,4},{6,5},{7,6},{9,8},{10,9},{11,10},{13,12},{... | collective-permute-start | bytes 3145736 | tf_op jit(solution)/shard_map/ppermute | solution.py:436
  159.6 3.4 %collective-permute-start.12 = (f32[2,512,128]{2,1,0:T(8,128)}, f32[2,512,128]{2,1,0:T(8,128)}, u32[]{:S(2)}, u32[]{:S(2)}) collective-permute-start(f32[2,512,128]{2,1,0:T(8,128)} %get-tuple-element.194), channel_id=1, source_target_pairs={{0,4},{1,5},{2,6},{3,7},{4,8},{5,9},{6,10},{7,11},{8,12},{9,13},{1... | collective-permute-start | bytes 1572872 | tf_op jit(solution)/shard_map/ppermute | solution.py:436
  163.0 3.2 %collective-permute-start.13 = (f32[2,512,128]{2,1,0:T(8,128)}, f32[2,512,128]{2,1,0:T(8,128)}, u32[]{:S(2)}, u32[]{:S(2)}) collective-permute-start(f32[2,512,128]{2,1,0:T(8,128)} %get-tuple-element.195), channel_id=1, source_target_pairs={{4,0},{5,1},{6,2},{7,3},{8,4},{9,5},{10,6},{11,7},{12,8},{13,9},{1... | collective-permute-start | bytes 1572872 | tf_op jit(solution)/shard_map/ppermute | solution.py:436
  166.3 8.1 %all-to-all-done.4 = f32[32,24,256]{2,1,0:T(8,128)S(1)} async-done(((f32[32,24,256]{2,1,0:T(8,128)}), f32[32,24,256]{2,1,0:T(8,128)S(1)}, u32[]{:S(2)}, u32[]{:S(2)}) %all-to-all-start.4) | async-done | bytes 786464 | tf_op jit(solution)/shard_map/all_to_all | solution.py:508
  176.5 5.8 %all-to-all-start.5 = ((f32[32,16,256]{2,1,0:T(8,128)}), f32[32,16,256]{2,1,0:T(8,128)S(1)}, u32[]{:S(2)}, u32[]{:S(2)}) async-start(f32[32,16,256]{2,1,0:T(8,128)} %broadcast_in_dim.7), calls=%async_computation.5 | async-start | bytes 1048576 | tf_op jit(solution)/shard_map/all_to_all | solution.py:516
  182.3 10.8 %collective-permute-done.12.west = f32[2,512,128]{2,1,0:T(8,128)} collective-permute-done((f32[2,512,128]{2,1,0:T(8,128)}, f32[2,512,128]{2,1,0:T(8,128)}, u32[]{:S(2)}, u32[]{:S(2)}) %collective-permute-start.12) | collective-permute-done | bytes 524320 | tf_op jit(solution)/shard_map/ppermute | solution.py:436
  198.4 3.1 %collective-permute-start.14 = (f32[2,128,256]{2,1,0:T(8,128)}, f32[2,128,256]{2,1,0:T(8,128)}, u32[]{:S(2)}, u32[]{:S(2)}) collective-permute-start(f32[2,128,256]{2,1,0:T(8,128)} %pad_maximum_fusion.5), channel_id=1, source_target_pairs={{0,1},{1,2},{2,3},{4,5},{5,6},{6,7},{8,9},{9,10},{10,11},{12,13},{... | collective-permute-start | bytes 786440 | tf_op jit(solution)/shard_map/ppermute | solution.py:436
  202.9 3.5 %collective-permute-done.14.top = f32[2,128,256]{2,1,0:T(8,128)} collective-permute-done((f32[2,128,256]{2,1,0:T(8,128)}, f32[2,128,256]{2,1,0:T(8,128)}, u32[]{:S(2)}, u32[]{:S(2)}) %collective-permute-start.14) | collective-permute-done | bytes 262176 | tf_op jit(solution)/shard_map/ppermute | solution.py:436
  206.4 4.6 %shard_map.112 = f32[2,256,1024]{2,1,0:T(8,128)} custom-call(f32[2,256,1024]{2,1,0:T(8,128)} %get-tuple-element.189.middle, f32[2,128,1024]{2,1,0:T(8,128)} %collective-permute-done.10.north, f32[2,128,1024]{2,1,0:T(8,128)} %collective-permute-done.11.south, f32[2,512,128]{2,1,0:T(8,128)} %collective-permute-done.12.west, ...), custom_call_target="tpu_custom_call" | custom-call | tf_op jit(solution)/shard_map/pallas_call | solution.py:463
  (40 shorter events, 22.3 us)
Async XLA Ops:
  7.2 6.4 %copy-start = (f32[2,256,1024]{2,1,0:T(8,128)S(1)}, f32[2,256,1024]{2,1,0:T(8,128)}, u32[]{:S(2)}) copy-start(f32[2,256,1024]{2,1,0:T(8,128)} %refs_2_.2) | copy-start | bytes 6291460
  7.2 76.2 %all-gather.3.cloned.1.call-start = ((), (), s32[]{:S(2)}) async-start(), calls=%async_computation.6 | async-start | bytes 2506752 | tf_op jit(solution)/shard_map/all_gather | solution.py:498
  12.8 4.4 %copy-start.2 = (bf16[8,272,256]{2,1,0:T(8,128)(2,1)}, bf16[8,272,256]{2,1,0:T(8,128)(2,1)S(1)}, u32[]{:S(2)}) copy-start(bf16[8,272,256]{2,1,0:T(8,128)(2,1)S(1)} %get-tuple-element.172) | copy-start | bytes 3342340
  13.6 18.0 %collective-permute-start.6 = (f32[2,256,128]{2,1,0:T(8,128)S(1)}, f32[2,256,128]{2,1,0:T(8,128)S(1)}, u32[]{:S(2)}, u32[]{:S(2)}) collective-permute-start(f32[2,256,128]{2,1,0:T(8,128)S(1)} %get-tuple-element.243), channel_id=1, source_target_pairs={{0,4},{1,5},{2,6},{3,7},{4,8},{5,9},{6,10},{7,11},{8,12},{9,13},{1... | collective-permute-start | bytes 786440 | tf_op jit(solution)/shard_map/ppermute | solution.py:436
  17.1 14.5 %collective-permute-start.7 = (f32[2,256,128]{2,1,0:T(8,128)S(1)}, f32[2,256,128]{2,1,0:T(8,128)}, u32[]{:S(2)}, u32[]{:S(2)}) collective-permute-start(f32[2,256,128]{2,1,0:T(8,128)S(1)} %get-tuple-element.242), channel_id=1, source_target_pairs={{4,0},{5,1},{6,2},{7,3},{8,4},{9,5},{10,6},{11,7},{12,8},{13,9},{1... | collective-permute-start | bytes 786440 | tf_op jit(solution)/shard_map/ppermute | solution.py:436
  31.7 10.4 %copy-start.6 = (f32[2,256,128]{2,1,0:T(8,128)}, f32[2,256,128]{2,1,0:T(8,128)S(1)}, u32[]{:S(2)}) copy-start(f32[2,256,128]{2,1,0:T(8,128)S(1)} %collective-permute-done.6.west_ref.refs_4_.refs_3_) | copy-start | bytes 786436
  31.7 51.8 %all-to-all-start.3 = ((bf16[8,272,256]{2,1,0:T(8,128)(2,1)}), bf16[8,272,256]{2,1,0:T(8,128)(2,1)}, u32[]{:S(2)}, u32[]{:S(2)}) async-start(bf16[8,272,256]{2,1,0:T(8,128)(2,1)} %get-tuple-element.175), calls=%async_computation.3 | async-start | bytes 2228224 | tf_op jit(solution)/shard_map/all_to_all | solution.py:494
  42.1 17.3 %collective-permute-start.9 = (f32[2,128,1280]{2,1,0:T(8,128)}, f32[2,128,1280]{2,1,0:T(8,128)}, u32[]{:S(2)}, u32[]{:S(2)}) collective-permute-start(f32[2,128,1280]{2,1,0:T(8,128)} %pad_maximum_fusion.4), channel_id=1, source_target_pairs={{1,0},{2,1},{3,2},{5,4},{6,5},{7,6},{9,8},{10,9},{11,10},{13,12},{... | collective-permute-start | bytes 3932168 | tf_op jit(solution)/shard_map/ppermute | solution.py:436
  45.2 19.1 %collective-permute-start.8 = (f32[2,128,1280]{2,1,0:T(8,128)}, f32[2,128,1280]{2,1,0:T(8,128)S(1)}, u32[]{:S(2)}, u32[]{:S(2)}) collective-permute-start(f32[2,128,1280]{2,1,0:T(8,128)} %pad_maximum_fusion.3), channel_id=1, source_target_pairs={{0,1},{1,2},{2,3},{4,5},{5,6},{6,7},{8,9},{9,10},{10,11},{12,13},{... | collective-permute-start | bytes 3932168 | tf_op jit(solution)/shard_map/ppermute | solution.py:436
  64.3 51.5 %copy-start.3 = (f32[2,128,1280]{2,1,0:T(8,128)}, f32[2,128,1280]{2,1,0:T(8,128)S(1)}, u32[]{:S(2)}) copy-start(f32[2,128,1280]{2,1,0:T(8,128)S(1)} %collective-permute-done.8.north_ref.refs_6_.refs_5_) | copy-start | bytes 3932164
  83.4 32.3 %all-to-all-start.2 = ((bf16[8,272,256]{2,1,0:T(8,128)(2,1)}), bf16[8,272,256]{2,1,0:T(8,128)(2,1)}, u32[]{:S(2)}, u32[]{:S(2)}) async-start(bf16[8,272,256]{2,1,0:T(8,128)(2,1)} %get-tuple-element.177), calls=%async_computation.2 | async-start | bytes 2228224 | tf_op jit(solution)/shard_map/all_to_all | solution.py:502
  124.6 49.8 %all-to-all-start.4 = ((f32[32,24,256]{2,1,0:T(8,128)}), f32[32,24,256]{2,1,0:T(8,128)S(1)}, u32[]{:S(2)}, u32[]{:S(2)}) async-start(f32[32,24,256]{2,1,0:T(8,128)} %get-tuple-element.188), calls=%async_computation.4 | async-start | bytes 1572864 | tf_op jit(solution)/shard_map/all_to_all | solution.py:508
  154.0 21.6 %collective-permute-start.10 = (f32[2,128,1024]{2,1,0:T(8,128)}, f32[2,128,1024]{2,1,0:T(8,128)}, u32[]{:S(2)}, u32[]{:S(2)}) collective-permute-start(f32[2,128,1024]{2,1,0:T(8,128)} %get-tuple-element.190), channel_id=1, source_target_pairs={{0,1},{1,2},{2,3},{4,5},{5,6},{6,7},{8,9},{9,10},{10,11},{12,13},{... | collective-permute-start | bytes 3145736 | tf_op jit(solution)/shard_map/ppermute | solution.py:436
  156.1 19.5 %collective-permute-start.11 = (f32[2,128,1024]{2,1,0:T(8,128)}, f32[2,128,1024]{2,1,0:T(8,128)}, u32[]{:S(2)}, u32[]{:S(2)}) collective-permute-start(f32[2,128,1024]{2,1,0:T(8,128)} %get-tuple-element.191), channel_id=1, source_target_pairs={{1,0},{2,1},{3,2},{5,4},{6,5},{7,6},{9,8},{10,9},{11,10},{13,12},{... | collective-permute-start | bytes 3145736 | tf_op jit(solution)/shard_map/ppermute | solution.py:436
  159.6 33.4 %collective-permute-start.12 = (f32[2,512,128]{2,1,0:T(8,128)}, f32[2,512,128]{2,1,0:T(8,128)}, u32[]{:S(2)}, u32[]{:S(2)}) collective-permute-start(f32[2,512,128]{2,1,0:T(8,128)} %get-tuple-element.194), channel_id=1, source_target_pairs={{0,4},{1,5},{2,6},{3,7},{4,8},{5,9},{6,10},{7,11},{8,12},{9,13},{1... | collective-permute-start | bytes 1572872 | tf_op jit(solution)/shard_map/ppermute | solution.py:436
  163.0 31.0 %collective-permute-start.13 = (f32[2,512,128]{2,1,0:T(8,128)}, f32[2,512,128]{2,1,0:T(8,128)}, u32[]{:S(2)}, u32[]{:S(2)}) collective-permute-start(f32[2,512,128]{2,1,0:T(8,128)} %get-tuple-element.195), channel_id=1, source_target_pairs={{4,0},{5,1},{6,2},{7,3},{8,4},{9,5},{10,6},{11,7},{12,8},{13,9},{1... | collective-permute-start | bytes 1572872 | tf_op jit(solution)/shard_map/ppermute | solution.py:436
  176.5 34.5 %all-to-all-start.5 = ((f32[32,16,256]{2,1,0:T(8,128)}), f32[32,16,256]{2,1,0:T(8,128)S(1)}, u32[]{:S(2)}, u32[]{:S(2)}) async-start(f32[32,16,256]{2,1,0:T(8,128)} %broadcast_in_dim.7), calls=%async_computation.5 | async-start | bytes 1048576 | tf_op jit(solution)/shard_map/all_to_all | solution.py:516
  195.8 7.1 %collective-permute-start.15 = (f32[2,128,256]{2,1,0:T(8,128)}, f32[2,128,256]{2,1,0:T(8,128)}, u32[]{:S(2)}, u32[]{:S(2)}) collective-permute-start(f32[2,128,256]{2,1,0:T(8,128)} %pad_maximum_fusion.6), channel_id=1, source_target_pairs={{1,0},{2,1},{3,2},{5,4},{6,5},{7,6},{9,8},{10,9},{11,10},{13,12},{... | collective-permute-start | bytes 786440 | tf_op jit(solution)/shard_map/ppermute | solution.py:436
  198.4 8.0 %collective-permute-start.14 = (f32[2,128,256]{2,1,0:T(8,128)}, f32[2,128,256]{2,1,0:T(8,128)}, u32[]{:S(2)}, u32[]{:S(2)}) collective-permute-start(f32[2,128,256]{2,1,0:T(8,128)} %pad_maximum_fusion.5), channel_id=1, source_target_pairs={{0,1},{1,2},{2,3},{4,5},{5,6},{6,7},{8,9},{9,10},{10,11},{12,13},{... | collective-permute-start | bytes 786440 | tf_op jit(solution)/shard_map/ppermute | solution.py:436
  206.4 4.6 %copy-start.7 = (f32[2,256,128]{2,1,0:T(8,128)S(1)}, f32[2,256,128]{2,1,0:T(8,128)}, u32[]{:S(2)}) copy-start(f32[2,256,128]{2,1,0:T(8,128)} %copy-done.6) | copy-start | bytes 786436
Sparse Core Ops, SparseCore 0:
  13.7 69.6 all-gather.2
